TPU v7x, 32 devices: a whole 2x2x4 slice. The times are simulated.
32 devices in a mesh: ctx: 4 (over x, core), exp: 8 (over z, y).
Axes of the slice: x: 2, y: 2, z: 4, core: 2. Of those that a mesh axis runs over, the one named last changes fastest.
Arguments:
- queries: bfloat16 [8, 1024, 2048], P('exp', 'ctx'), may hold values from -5 to 5
- key_rows: bfloat16 [8, 1024, 2048], P('exp', 'ctx'), may hold values from -5 to 5
- value_rows: bfloat16 [8, 1024, 2048], P('exp', 'ctx'), may hold values from -6 to 6
- residual_in: bfloat16 [8, 1024, 2048], P('exp', 'ctx'), may hold values from -6 to 6
- norm_gain: float32 [2048], replicated, may hold values from 0.1 to 1.9
- routes: int32 [8, 1024, 2], P('exp', 'ctx'), may hold values from 0 to 7, all different within a row; in each aligned block of 256 rows (0 to 255, 256 to 511, ..., all dimensions but the last counted through in order) at most 80 rows name the same one
- gate_weights: float32 [8, 1024, 2], P('exp', 'ctx'), may hold values from 0.25 to 1
- gate_up_weight: bfloat16 [8, 2048, 2, 1024], P('exp', None, None, 'ctx'), may hold values from -0.125 to 0.125
- down_weight: bfloat16 [8, 1024, 2048], P('exp', 'ctx'), may hold values from -0.1875 to 0.1875
Outputs:
- layer_out: bfloat16 [8, 1024, 2048], P('exp', 'ctx')
Inputs may be any that keep to these rules, and one draw needn't show every extreme that they name: `routes`: within the rows of one device (aligned blocks of 256 tokens in clip-then-frame order), no expert is named more than 80 times; the 2 experts of a token differ.
All inputs are finite; a program needn't handle non-finite values.
Results may differ from a plain program's by a relative error of at most 0.011.
Values may be sent and summed in bfloat16 or wider, within the bound.
A program may use at most 128 MiB of HBM per device.

v0:
```python
import jax
import jax.numpy as jnp
from jax import lax
from jax.sharding import PartitionSpec as P

HEADS = 16


def shards(
    queries,
    key_rows,
    value_rows,
    residual_in,
    norm_gain,
    routes,
    gate_weights,
    gate_up_weight,
    down_weight,
):
    clip_count, row_count, feature_count = queries.shape
    head_count = HEADS
    head_size = feature_count // head_count
    score_scale = head_size ** (-0.5)
    query_heads = queries.reshape(clip_count, row_count, head_count, head_size)
    running_max = jnp.full((clip_count, row_count, head_count), -1e30, jnp.float32)
    key_part = lax.all_gather(key_rows, "ctx", axis=1, tiled=True)
    value_part = lax.all_gather(value_rows, "ctx", axis=1, tiled=True)
    key_heads = key_part.reshape(clip_count, -1, head_count, head_size)
    value_heads = value_part.reshape(clip_count, -1, head_count, head_size)
    scores = (
        jnp.einsum("cqhd,ckhd->cqhk", query_heads, key_heads, preferred_element_type=jnp.float32)
        * score_scale
    )
    new_max = jnp.maximum(running_max, jnp.max(scores, axis=-1))
    expo = jnp.exp(scores - new_max[..., None])
    running_sum = jnp.sum(expo, axis=-1)
    weighted = jnp.einsum(
        "cqhk,ckhd->cqhd",
        expo.astype(jnp.bfloat16),
        value_heads,
        preferred_element_type=jnp.float32,
    )
    final_max, final_sum, weighted = (new_max, running_sum, weighted)
    attention = (weighted / final_sum[..., None]).reshape(clip_count, row_count, feature_count)
    mixed_rows = (residual_in.astype(jnp.float32) + attention).astype(jnp.bfloat16)
    mixed_float = mixed_rows.astype(jnp.float32)
    mean_square = jnp.mean(mixed_float * mixed_float, axis=-1, keepdims=True)
    normed = (mixed_float * lax.rsqrt(mean_square + 1e-05) * norm_gain).astype(jnp.bfloat16)
    token_count = clip_count * row_count
    top_count = routes.shape[-1]
    expert_count = lax.axis_size("exp") * gate_up_weight.shape[0]
    capacity = max(2, -(-(5 * token_count * top_count) // (4 * expert_count)))
    flat_routes = routes.reshape(-1)
    one_hot = (flat_routes[:, None] == jnp.arange(expert_count, dtype=jnp.int32)[None, :]).astype(
        jnp.int32
    )
    running_count = jnp.cumsum(one_hot, axis=0)
    slot_index = jnp.sum(running_count * one_hot, axis=1) - 1
    destination = flat_routes * capacity + slot_index
    source_rows = jnp.repeat(normed.reshape(token_count, feature_count), top_count, axis=0)
    send_buffer = (
        jnp.zeros((expert_count * capacity, feature_count), jnp.bfloat16)
        .at[destination]
        .set(source_rows)
    )
    send_buffer = send_buffer.reshape(expert_count, capacity, feature_count)
    local_units = down_weight.shape[1]
    portion = lax.all_gather(
        lax.all_to_all(send_buffer, "exp", split_axis=0, concat_axis=0, tiled=True),
        "ctx",
        axis=1,
        tiled=True,
    )
    flattened = portion.reshape(-1, feature_count)
    gate_and_up = jnp.dot(
        flattened,
        gate_up_weight[0].reshape(feature_count, 2 * local_units),
        preferred_element_type=jnp.float32,
    )
    hidden = (jax.nn.silu(gate_and_up[:, :local_units]) * gate_and_up[:, local_units:]).astype(
        jnp.bfloat16
    )
    projected = jnp.dot(hidden, down_weight[0], preferred_element_type=jnp.float32)
    terms = projected.reshape(portion.shape[0], portion.shape[1], feature_count)
    summed = lax.psum_scatter(terms.astype(jnp.bfloat16), "ctx", scatter_dimension=1, tiled=True)
    returned = lax.all_to_all(summed, "exp", split_axis=0, concat_axis=0, tiled=True)
    expert_out = returned.reshape(-1, feature_count)[destination]
    expert_out = expert_out.reshape(token_count, top_count, feature_count).astype(jnp.float32)
    expert_sum = jnp.sum(gate_weights.reshape(token_count, top_count, 1) * expert_out, axis=1)
    layer_out = (mixed_float.reshape(token_count, feature_count) + expert_sum).astype(jnp.bfloat16)
    return layer_out.reshape(clip_count, row_count, feature_count)


def solution(mesh):
    return jax.shard_map(
        shards,
        mesh=mesh,
        in_specs=(
            P("exp", "ctx", None),
            P("exp", "ctx", None),
            P("exp", "ctx", None),
            P("exp", "ctx", None),
            P(),
            P("exp", "ctx", None),
            P("exp", "ctx", None),
            P("exp", None, None, "ctx"),
            P("exp", "ctx", None),
        ),
        out_specs=P("exp", "ctx", None),
        check_vma=False,
    )
```

profile of v0, /device:TPU:13, one launch (start us, length us, event | category | flops | bytes accessed | tf_op | source)
XLA Modules:
  0.0 441.6 jit_solution(7315403084919850439)
XLA Ops:
  6.5 2.4 copy.15
  12.3 33.4 %all-gather.4.cloned.1.call-done = bf16[1,1024,2048]{1,2,0:T(8,128)(2,1)} async-done(((bf16[1,256,2048]{1,2,0:T(8,128)(2,1)}), bf16[1,1024,2048]{1,2,0:T(8,128)(2,1)}) %all-gather.4.cloned.1.call-update) | async-done | bytes 4194320 | tf_op jit(solution)/shard_map/all_gather | solution.py:26
  45.7 11.6 %bitcast_reduce_fusion = (f32[256,16]{0,1:T(8,128)S(1)}, f32[16,1024,256]{2,1,0:T(8,128)}) fusion(bf16[1024,16,128]{0,2,1:T(8,128)(2,1)} %bitcast.66, bf16[256,16,128]{2,1,0:T(8,128)(2,1)S(1)} %bitcast.64), kind=kOutput, calls=%fused_computation.3 | convolution fusion | flops 1082126336 | bytes 22036480 | tf_op jit(solution)/shard_map/cqhd,ckhd->cqhk/dot_general | solution.py:31
  57.3 8.5 %fusion.1 = f32[256,16]{0,1:T(8,128)S(1)} fusion(f32[16,1024,256]{2,1,0:T(8,128)} %get-tuple-element.8, f32[256,16]{0,1:T(8,128)S(1)} %broadcast_maximum_fusion), kind=kLoop, calls=%fused_computation.5 | loop fusion | flops 12578816 | bytes 16809984 | tf_op jit(solution)/shard_map/reduce_sum | solution.py:36
  65.8 15.9 %all-gather.6.cloned.1.call-done = bf16[1,1024,2048]{2,1,0:T(8,128)(2,1)} async-done(((bf16[1,256,2048]{2,1,0:T(8,128)(2,1)}), bf16[1,1024,2048]{2,1,0:T(8,128)(2,1)}) %all-gather.6.cloned.1.call-update) | async-done | bytes 4194320 | tf_op jit(solution)/shard_map/all_gather | solution.py:27
  81.8 6.4 %copy.18 = bf16[1,1024,2048]{1,2,0:T(8,128)(2,1)} copy(bf16[1,1024,2048]{2,1,0:T(8,128)(2,1)} %all-gather.6.cloned.1.call-done) | data formatting | bytes 8388608 | tf_op jit(solution)/shard_map/all_gather | solution.py:27
  88.2 9.2 %bitcast_divide_fusion = f32[1,256,16,128]{1,3,2,0:T(8,128)S(1)} fusion(bf16[1024,16,128]{0,2,1:T(8,128)(2,1)} %bitcast.65, f32[16,1024,256]{2,1,0:T(8,128)} %get-tuple-element.8, f32[256,16]{0,1:T(8,128)S(1)} %broadcast_maximum_fusion, f32[256,16]{0,1:T(8,128)S(1)} %fusion.1), kind=kOutput, calls=%fused_computation.22 | convolution fusion | flops 1086849024 | bytes 23101440 | tf_op jit(solution)/shard_map/cqhk,ckhd->cqhd/dot_general | solution.py:37
  97.4 1.9 copy.20
  99.3 2.3 fusion.9
  101.9 2.6 broadcast_in_dim.8
  104.5 4.1 reshape.155
  108.6 6.6 %scatter_custom_fusion = bf16[640,2048]{1,0:T(8,128)(2,1)} fusion(s32[512]{0:T(512)S(1)} %bitcast.71, bf16[512,2048]{1,0:T(8,128)(2,1)} %reshape.155, bf16[]{:T(256)} %constant.8.clone.1), kind=kCustom, calls=%fused_computation.24 | custom fusion | bytes 2621952 | tf_op jit(solution)/shard_map/scatter | solution.py:64
  115.2 62.2 %all_to_all.10 = bf16[8,80,2048]{2,1,0:T(8,128)(2,1)} all-to-all(bf16[8,80,2048]{2,1,0:T(8,128)(2,1)} %bitcast.62), channel_id=1, replica_groups=mesh['ctx'=4,'exp'=8] {'exp'}, dimensions={0} | all-to-all | bytes 5242880 | tf_op jit(solution)/shard_map/all_to_all | solution.py:69
  177.5 3.3 copy.28
  180.8 68.4 %all-gather.8.cloned.1.call-done = bf16[8,320,2048]{2,1,0:T(8,128)(2,1)} async-done(((bf16[8,80,2048]{2,1,0:T(8,128)(2,1)}), bf16[8,320,2048]{2,1,0:T(8,128)(2,1)}) %all-gather.8.cloned.1.call-update) | async-done | bytes 10485776 | tf_op jit(solution)/shard_map/all_gather | solution.py:68
  249.2 9.0 %fusion.24 = f32[2560,512]{1,0:T(8,128)S(1)} fusion(bf16[2560,2048]{1,0:T(8,128)(2,1)} %bitcast.75, bf16[2048,512]{1,0:T(8,128)(2,1)} %bitcast.68), kind=kOutput, calls=%fused_computation.43 | convolution fusion | flops 5368709120 | bytes 17825792 | tf_op jit(solution)/shard_map/dot_general | solution.py:75
  259.1 5.5 %convolution_convert_fusion = bf16[8,320,2048]{2,1,0:T(8,128)(2,1)} fusion(bf16[8,320,256]{2,1,0:T(8,128)(2,1)S(1)} %bitcast.63, bf16[1,256,2048]{2,1,0:T(8,128)(2,1)S(1)} %copy-done), kind=kOutput, calls=%fused_computation.11 | convolution fusion | flops 2689597440 | bytes 12845056 | tf_op jit(solution)/shard_map/dot_general | solution.py:83
  264.6 85.0 %reduce-scatter.2.cloned.1.call-done = bf16[8,80,2048]{2,1,0:T(8,128)(2,1)} async-done(((bf16[8,320,2048]{2,1,0:T(8,128)(2,1)}), bf16[8,80,2048]{2,1,0:T(8,128)(2,1)}) %reduce-scatter.2.cloned.1.call-update) | async-done | bytes 2621456 | tf_op jit(solution)/shard_map/reduce_scatter | solution.py:85
  349.6 5.5 %all-to-all-start.1 = ((bf16[8,80,2048]{2,1,0:T(8,128)(2,1)}), bf16[8,80,2048]{2,1,0:T(8,128)(2,1)}, u32[]{:S(2)}, u32[]{:S(2)}) async-start(bf16[8,80,2048]{2,1,0:T(8,128)(2,1)} %reduce-scatter.2.cloned.1.call-done), calls=%async_computation.2 | async-start | bytes 5242880 | tf_op jit(solution)/shard_map/all_to_all | solution.py:86
  355.3 56.8 %all-to-all-done.1 = bf16[8,80,2048]{2,1,0:T(8,128)(2,1)} async-done(((bf16[8,80,2048]{2,1,0:T(8,128)(2,1)}), bf16[8,80,2048]{2,1,0:T(8,128)(2,1)}, u32[]{:S(2)}, u32[]{:S(2)}) %all-to-all-start.1) | async-done | bytes 2621472 | tf_op jit(solution)/shard_map/all_to_all | solution.py:86
  412.1 7.3 %gather_fusion = bf16[512,2048]{1,0:T(8,128)(2,1)} fusion(bf16[640,2048]{1,0:T(8,128)(2,1)} %bitcast.21, s32[1024]{0:T(1024)S(1)} %pad_clamp_fusion), kind=kCustom, calls=%fused_computation | custom fusion | bytes 4196352 | tf_op jit(solution)/shard_map/gather | solution.py:87
  419.4 5.4 %reshape.142 = f32[256,2,2048]{2,1,0:T(2,128)} reshape(bf16[512,2048]{1,0:T(8,128)(2,1)} %gather_fusion) | data formatting | bytes 6291456 | tf_op jit(solution)/shard_map/convert_element_type | solution.py:88
  424.9 8.9 %multiply_reduce_fusion = f32[256,2048]{1,0:T(8,128)S(1)} fusion(f32[256,2,2048]{2,1,0:T(2,128)} %reshape.142, f32[256,2]{1,0:T(8,128)S(1)} %copy.21), kind=kLoop, calls=%fused_computation.12 | loop fusion | flops 1572864 | bytes 6293504 | tf_op jit(solution)/shard_map/reduce_sum | solution.py:89
  433.8 1.3 fusion.12
  (39 shorter events, 4.6 us)
Async XLA Ops:
  6.5 252.5 %copy-start = (bf16[1,256,2048]{2,1,0:T(8,128)(2,1)S(1)}, bf16[1,256,2048]{2,1,0:T(8,128)(2,1)}, u32[]{:S(2)}) copy-start(bf16[1,256,2048]{2,1,0:T(8,128)(2,1)} %param.17) | copy-start | bytes 3145732
  6.5 3.2 copy-start.3
  6.5 3.7 copy-start.1
  6.5 39.2 %all-gather.4.cloned.1.call-start = ((), (), s32[]{:S(2)}) async-start(), calls=%async_computation.3 | async-start | bytes 5242880 | tf_op jit(solution)/shard_map/all_gather | solution.py:26
  9.0 72.8 %all-gather.6.cloned.1.call-start = ((), (), s32[]{:S(2)}) async-start(), calls=%async_computation.4 | async-start | bytes 5242880 | tf_op jit(solution)/shard_map/all_gather | solution.py:27
  9.7 239.5 %all-gather.8.cloned.1.call-start = ((), (), s32[]{:S(2)}) async-start(), calls=%async_computation.5 | async-start | bytes 13107200 | tf_op jit(solution)/shard_map/all_gather | solution.py:68
  99.3 2.3 copy-start.2
  177.4 172.2 %reduce-scatter.2.cloned.1.call-start = ((), (), s32[]{:S(2)}) async-start(), calls=%async_computation.6 | async-start | bytes 13107200 | tf_op jit(solution)/shard_map/reduce_scatter | solution.py:85
  264.6 90.5 %copy-start.4 = (f32[1,256,2]{1,2,0:T(2,128)S(1)}, f32[1,256,2]{1,2,0:T(2,128)}, u32[]{:S(2)}) copy-start(f32[1,256,2]{1,2,0:T(2,128)} %param.15) | copy-start | bytes 6148
  349.6 62.4 %all-to-all-start.1 = ((bf16[8,80,2048]{2,1,0:T(8,128)(2,1)}), bf16[8,80,2048]{2,1,0:T(8,128)(2,1)}, u32[]{:S(2)}, u32[]{:S(2)}) async-start(bf16[8,80,2048]{2,1,0:T(8,128)(2,1)} %reduce-scatter.2.cloned.1.call-done), calls=%async_computation.2 | async-start | bytes 5242880 | tf_op jit(solution)/shard_map/all_to_all | solution.py:86
Sparse Core Ops, SparseCore 0:
  9.1 36.5 all-gather.3
  47.3 34.4 all-gather.5
  177.6 71.6 all-gather.7
  264.7 84.8 reduce-scatter.1
where the time goes:
time: 447 us; the launch traced here: 442 us
  waiting for transfers between devices  260 us (58%)
  blocking collectives  62.2 us (14%)
  local copies, waits for them, and re-layouts  41.5 us (9%)
  matrix products  35.3 us (8%)
  other arithmetic  23.5 us (5%)
  between operations  13.3 us (3%)
  starting transfers between devices  5.61 us (1%)
    reduce_scatter x1, waiting for transfers between devices, shards(): lax.psum_scatter(terms.astype(jnp.bfloat16), 'ctx', scatter_dimension=1,...  85 us
    all_gather x1, waiting for transfers between devices, shards(): lax.all_gather(lax.all_to_all(send_buffer, 'exp', split_axis=0, concat_ax...  68.4 us
    all_to_all x1, blocking collectives, shards(): lax.all_to_all(send_buffer, 'exp', split_axis=0, concat_axis=0, tiled=True)  62.2 us
    all_to_all x1, waiting for transfers between devices, shards(): lax.all_to_all(summed, 'exp', split_axis=0, concat_axis=0, tiled=True)  56.8 us
    all_gather x1, waiting for transfers between devices, shards(): key_part = lax.all_gather(key_rows, 'ctx', axis=1, tiled=True)  33.4 us
    all_gather x1, waiting for transfers between devices, shards(): value_part = lax.all_gather(value_rows, 'ctx', axis=1, tiled=True)  15.9 us
    dot_general x1, matrix products, shards(): jnp.einsum('cqhd,ckhd->cqhk', query_heads, key_heads, preferred_element_t...  11.6 us
    dot_general x1, matrix products, shards(): jnp.einsum('cqhk,ckhd->cqhd', expo.astype(jnp.bfloat16), value_heads, pre...  9.22 us
  transfers between devices with their start and end apart: 5, of which 5 were waited for; matrix products, arithmetic and copies ran while one was open for 6% of the time, Pallas kernels for 0%

commit v1 on v0

v1 whole, which is shorter than its diff:
```python
import functools

import jax
import jax.numpy as jnp
from jax import lax
from jax.experimental import pallas as pl
from jax.experimental.pallas import tpu as pltpu
from jax.sharding import PartitionSpec as P

HEADS = 16
MESH = pl.DeviceIdType.MESH
F32 = jnp.float32
BF16 = jnp.bfloat16
OWN, CORE, CHIP, FAR = range(4)
TILE = 512


def flipped(index, offset, extent):
    result = jnp.int32(0)
    bit = 1
    while bit < extent:
        both = lax.div(index, jnp.int32(bit)) + lax.div(jnp.int32(offset), jnp.int32(bit))
        result = result + lax.rem(both, jnp.int32(2)) * bit
        bit *= 2
    return result


def rows_at(start, count):
    return pl.ds(pl.multiple_of(start, 16), count)


def columns_at(step, width):
    return pl.ds(pl.multiple_of(step * width, width), width)


def layer_kernel(
    n_exp, cap, chunk, scale,
    q_ref, k_ref, v_ref, residual_ref, gain_ref, routes_ref, routes_t_ref, gates_ref, gu_ref, dn_ref,
    out_ref,
    q_buf, k_buf, v_buf, residual_buf, mixed, normed, gu_buf, dn_buf,
    pick, place, send_buf, recv_buf, hidden, result_buf, back_buf,
    local_sem, kv_send, kv_recv, w_send, w_recv, out_send, out_recv, back_send, back_recv,
):
    tokens, features = q_ref.shape
    top = gates_ref.shape[1]
    units = dn_ref.shape[0]
    slots = send_buf.shape[0]
    chunks = features // chunk
    half = n_exp // 2
    half_rows = half * cap
    ctx = lax.axis_index("ctx")
    me = lax.axis_index("exp")
    core_peer = flipped(ctx, 1, 4)
    chip_peer = flipped(ctx, 2, 4)
    far_peer = flipped(ctx, 3, 4)

    local = [
        pltpu.make_async_copy(src, dst, local_sem.at[i])
        for i, (src, dst) in enumerate(
            [
                (q_ref, q_buf),
                (k_ref, k_buf.at[pl.ds(0, tokens)]),
                (v_ref, v_buf.at[pl.ds(0, tokens)]),
                (residual_ref, residual_buf),
                (gu_ref, gu_buf.at[OWN]),
                (dn_ref, dn_buf.at[pl.ds(0, units)]),
            ]
        )
    ]
    for copy in local:
        copy.start()

    barrier = pltpu.get_barrier_semaphore()
    for peer in (core_peer, chip_peer, far_peer):
        pl.semaphore_signal(barrier, inc=1, device_id={"ctx": peer}, device_id_type=MESH)

    @pl.loop(1, n_exp)
    def _(d):
        pl.semaphore_signal(
            barrier, inc=1, device_id={"exp": flipped(me, d, n_exp)}, device_id_type=MESH
        )

    pl.semaphore_wait(barrier, 3 + n_exp - 1)

    def kv_copy(kind, route, g):
        src, buf = ((k_ref, k_buf), (v_ref, v_buf))[kind]
        cols = columns_at(g, chunk)
        if route == FAR:
            block = buf.at[pl.ds(CHIP * tokens, tokens), cols]
        else:
            block = src.at[:, cols]
        return pltpu.make_async_remote_copy(
            src_ref=block,
            dst_ref=buf.at[pl.ds(route * tokens, tokens), cols],
            send_sem=kv_send.at[kind, route - 1, g],
            recv_sem=kv_recv.at[kind, route - 1, g],
            device_id={"ctx": chip_peer if route == CHIP else core_peer},
            device_id_type=MESH,
        )

    gu_pieces, dn_pieces = 4, 2
    pieces = gu_pieces + dn_pieces

    def weight_copy(route, i):
        if i < gu_pieces:
            size = features // gu_pieces
            part = pl.ds(i * size, size)
            src, dst = gu_ref.at[part], gu_buf.at[route, part]
            held = gu_buf.at[CHIP, part]
        else:
            size = units // dn_pieces
            start = (i - gu_pieces) * size
            src = dn_ref.at[pl.ds(start, size)]
            dst = dn_buf.at[pl.ds(route * units + start, size)]
            held = dn_buf.at[pl.ds(CHIP * units + start, size)]
        return pltpu.make_async_remote_copy(
            src_ref=held if route == FAR else src,
            dst_ref=dst,
            send_sem=w_send.at[route - 1, i],
            recv_sem=w_recv.at[route - 1, i],
            device_id={"ctx": chip_peer if route == CHIP else core_peer},
            device_id_type=MESH,
        )

    @pl.loop(0, chunks)
    def _(g):
        for kind in range(2):
            kv_copy(kind, CHIP, g).start()
            kv_copy(kind, CORE, g).start()

    for i in range(pieces):
        weight_copy(CORE, i).start()

    expert_lane = lax.broadcasted_iota(jnp.int32, (tokens, 128), 1)
    named = [routes_ref[:, j : j + 1] == expert_lane for j in range(top)]
    counted = sum(jnp.where(hit, 1.0, 0.0) for hit in named).astype(BF16)
    row = lax.broadcasted_iota(jnp.int32, (tokens, tokens), 0)
    col = lax.broadcasted_iota(jnp.int32, (tokens, tokens), 1)
    earlier = jnp.where(row > col, 1.0, 0.0).astype(BF16)
    slot = jnp.dot(earlier, counted, preferred_element_type=F32) + (expert_lane * cap).astype(F32)
    slot_lane = lax.broadcasted_iota(jnp.int32, (tokens, slots), 1).astype(F32)
    for j in range(top):
        target = jnp.sum(jnp.where(named[j], slot, 0.0), axis=1, keepdims=True)
        pick[j] = jnp.where(target == slot_lane, 1.0, 0.0).astype(BF16)

    expert_row = lax.broadcasted_iota(jnp.int32, (128, tokens), 0)
    named_t = [routes_t_ref[j : j + 1, :] == expert_row for j in range(top)]
    counted_t = sum(jnp.where(hit, 1.0, 0.0) for hit in named_t).astype(BF16)
    earlier_t = jnp.where(row < col, 1.0, 0.0).astype(BF16)
    slot_t = jnp.dot(counted_t, earlier_t, preferred_element_type=F32) + (expert_row * cap).astype(F32)
    slot_row = lax.broadcasted_iota(jnp.int32, (slots, tokens), 0).astype(F32)
    placed = jnp.zeros((slots, tokens), F32)
    for j in range(top):
        target = jnp.sum(jnp.where(named_t[j], slot_t, 0.0), axis=0, keepdims=True)
        placed = placed + jnp.where(target == slot_row, 1.0, 0.0)
    place[...] = placed.astype(BF16)

    for copy in local:
        copy.wait()

    @pl.loop(0, chunks + 1)
    def _(g):
        @pl.when(g < chunks)
        def _():
            for kind in range(2):
                kv_copy(kind, CHIP, g).wait_recv()
                kv_copy(kind, FAR, g).start()

        @pl.when(g == chunks - 2)
        def _():
            for i in range(pieces):
                weight_copy(CHIP, i).start()

        @pl.when(g > 0)
        def _():
            done = g - 1
            for kind in range(2):
                kv_copy(kind, CORE, done).wait_recv()
                kv_copy(kind, FAR, done).wait_recv()
            for h in range(chunk // 128):
                cols = pl.ds(pl.multiple_of(done * chunk + h * 128, 128), 128)
                scores = (
                    lax.dot_general(
                        q_buf[:, cols], k_buf[:, cols], (((1,), (1,)), ((), ())),
                        preferred_element_type=F32,
                    )
                    * scale
                )
                expo = jnp.exp(scores - jnp.max(scores, axis=1, keepdims=True))
                total = jnp.sum(expo, axis=1, keepdims=True)
                weighted = jnp.dot(expo.astype(BF16), v_buf[:, cols], preferred_element_type=F32)
                mixed[:, cols] = (residual_buf[:, cols].astype(F32) + weighted / total).astype(BF16)

    @pl.loop(0, tokens // 32)
    def _(i):
        part = rows_at(i * 32, 32)
        value = mixed[part, :].astype(F32)
        mean_square = jnp.mean(value * value, axis=1, keepdims=True)
        normed[part, :] = (value * lax.rsqrt(mean_square + 1e-05) * gain_ref[...]).astype(BF16)

    def out_copy(d):
        return pltpu.make_async_remote_copy(
            src_ref=send_buf.at[rows_at(flipped(me, d, n_exp) * cap, cap)],
            dst_ref=recv_buf.at[rows_at(d * cap, cap)],
            send_sem=out_send.at[d],
            recv_sem=out_recv.at[d],
            device_id={"exp": flipped(me, d, n_exp)},
            device_id_type=MESH,
        )

    def back_copy(d):
        return pltpu.make_async_remote_copy(
            src_ref=result_buf.at[rows_at(d * cap, cap)],
            dst_ref=back_buf.at[rows_at(me * cap, cap)],
            send_sem=back_send.at[d],
            recv_sem=back_recv.at[d],
            device_id={"exp": flipped(me, d, n_exp)},
            device_id_type=MESH,
        )

    my_half = lax.div(me, jnp.int32(half))
    for which in (1, 0):
        part = rows_at(lax.rem(my_half + which, jnp.int32(2)) * half_rows, half_rows)

        @pl.loop(0, features // TILE)
        def _(t):
            cols = columns_at(t, TILE)
            send_buf[part, cols] = jnp.dot(
                place[part, :], normed[:, cols], preferred_element_type=F32
            ).astype(BF16)

        @pl.loop(max(1, which * half), which * half + half)
        def _(d):
            out_copy(d).start()

    recv_buf[pl.ds(0, cap), :] = send_buf[rows_at(me * cap, cap), :]

    for i in range(pieces):
        weight_copy(CHIP, i).wait_recv()
        weight_copy(FAR, i).start()
    for i in range(pieces):
        weight_copy(CORE, i).wait_recv()
        weight_copy(FAR, i).wait_recv()

    for which in (0, 1):
        part = pl.ds(which * half_rows, half_rows)

        @pl.loop(max(1, which * half), which * half + half)
        def _(d):
            out_copy(d).wait_recv()

        @pl.loop(0, 4)
        def _(r):
            both = jnp.dot(recv_buf[part, :], gu_buf[r], preferred_element_type=F32)
            gate, up = both[:, :units], both[:, units:]
            hidden[:, columns_at(r, units)] = (gate / (1.0 + jnp.exp(-gate)) * up).astype(BF16)

        @pl.loop(0, features // TILE)
        def _(t):
            cols = columns_at(t, TILE)
            result_buf[part, cols] = jnp.dot(
                hidden[...], dn_buf[:, cols], preferred_element_type=F32
            ).astype(BF16)

        @pl.loop(max(1, which * half), which * half + half)
        def _(d):
            back_copy(d).start()

    back_buf[rows_at(me * cap, cap), :] = result_buf[pl.ds(0, cap), :]

    @pl.loop(1, n_exp)
    def _(d):
        back_copy(d).wait_recv()

    @pl.loop(0, features // TILE)
    def _(t):
        cols = columns_at(t, TILE)
        total = mixed[:, cols].astype(F32)
        for j in range(top):
            routed = jnp.dot(pick[j], back_buf[:, cols], preferred_element_type=F32)
            total = total + gates_ref[:, j : j + 1] * routed
        out_ref[:, cols] = total.astype(BF16)

    @pl.loop(1, n_exp)
    def _(d):
        out_copy(d).wait_send()
        back_copy(d).wait_send()

    @pl.loop(0, chunks)
    def _(g):
        for kind in range(2):
            for route in (CORE, CHIP, FAR):
                kv_copy(kind, route, g).wait_send()

    for i in range(pieces):
        for route in (CORE, CHIP, FAR):
            weight_copy(route, i).wait_send()


def shards(
    queries,
    key_rows,
    value_rows,
    residual_in,
    norm_gain,
    routes,
    gate_weights,
    gate_up_weight,
    down_weight,
):
    clip_count, row_count, feature_count = queries.shape
    tokens = clip_count * row_count
    top = routes.shape[-1]
    n_exp = lax.axis_size("exp")
    n_ctx = lax.axis_size("ctx")
    units = down_weight.shape[1]
    assert clip_count == 1 and n_ctx == 4 and gate_up_weight.shape[0] == 1
    assert n_exp & (n_exp - 1) == 0 and feature_count == HEADS * 128
    capacity = max(2, -(-(5 * tokens * top) // (4 * n_exp)))
    cap = -(-capacity // 16) * 16
    slots = n_exp * cap
    chunk = 256
    chunks = feature_count // chunk
    flat = (tokens, feature_count)
    flat_routes = routes.reshape(tokens, top)
    anywhere = pl.BlockSpec(memory_space=pl.ANY)
    vmem = pl.BlockSpec(memory_space=pltpu.VMEM)
    dma = pltpu.SemaphoreType.DMA
    out = pl.pallas_call(
        functools.partial(layer_kernel, n_exp, cap, chunk, (feature_count // HEADS) ** (-0.5)),
        out_shape=jax.ShapeDtypeStruct(flat, BF16),
        in_specs=[anywhere] * 4 + [vmem] * 4 + [anywhere] * 2,
        out_specs=vmem,
        scratch_shapes=[
            pltpu.VMEM(flat, BF16),
            pltpu.VMEM((n_ctx * tokens, feature_count), BF16),
            pltpu.VMEM((n_ctx * tokens, feature_count), BF16),
            pltpu.VMEM(flat, BF16),
            pltpu.VMEM(flat, BF16),
            pltpu.VMEM(flat, BF16),
            pltpu.VMEM((n_ctx, feature_count, 2 * units), BF16),
            pltpu.VMEM((n_ctx * units, feature_count), BF16),
            pltpu.VMEM((top, tokens, slots), BF16),
            pltpu.VMEM((slots, tokens), BF16),
            pltpu.VMEM((slots, feature_count), BF16),
            pltpu.VMEM((slots, feature_count), BF16),
            pltpu.VMEM((slots // 2, n_ctx * units), BF16),
            pltpu.VMEM((slots, feature_count), BF16),
            pltpu.VMEM((slots, feature_count), BF16),
            dma((6,)),
            dma((2, 3, chunks)),
            dma((2, 3, chunks)),
            dma((3, 6)),
            dma((3, 6)),
            dma((n_exp,)),
            dma((n_exp,)),
            dma((n_exp,)),
            dma((n_exp,)),
        ],
        compiler_params=pltpu.CompilerParams(
            collective_id=0, has_side_effects=True, vmem_limit_bytes=60 * 1024 * 1024
        ),
        cost_estimate=pl.CostEstimate(
            flops=10_000_000_000, bytes_accessed=20_000_000, transcendentals=5_000_000
        ),
    )(
        queries.reshape(flat),
        key_rows.reshape(flat),
        value_rows.reshape(flat),
        residual_in.reshape(flat),
        norm_gain.reshape(1, feature_count),
        flat_routes,
        flat_routes.T,
        gate_weights.reshape(tokens, top),
        gate_up_weight.reshape(feature_count, 2 * units),
        down_weight.reshape(units, feature_count),
    )
    return out.reshape(clip_count, row_count, feature_count)


def solution(mesh):
    return jax.shard_map(
        shards,
        mesh=mesh,
        in_specs=(
            P("exp", "ctx", None),
            P("exp", "ctx", None),
            P("exp", "ctx", None),
            P("exp", "ctx", None),
            P(),
            P("exp", "ctx", None),
            P("exp", "ctx", None),
            P("exp", None, None, "ctx"),
            P("exp", "ctx", None),
        ),
        out_specs=P("exp", "ctx", None),
        check_vma=False,
    )
```

time: 447 us -> 203 us (0.45); the launches traced: 442 us -> 202 us
  waiting for transfers between devices: 260 us -> 0 us
  Pallas kernels: 0 us -> 194 us
  blocking collectives: 62.2 us -> 0 us
  matrix products: 35.3 us -> 0 us
  local copies, waits for them, and re-layouts: 41.5 us -> 8.63 us
  other arithmetic: 23.5 us -> 0 us
  between operations: 13.3 us -> 0.01 us
  starting transfers between devices: 5.61 us -> 0 us
    pallas_call x0 -> x1, Pallas kernels: none -> 194 us  [shards(): pl.pallas_call(functools.partial(layer_kernel, n_exp, cap, chunk, (featur...]
    all_gather x3 -> x0, waiting for transfers between devices: 118 us -> none  [the longest x1 68.4 us: shards(): lax.all_gather(lax.all_to_all(send_buffer, 'exp', split_axis=0, concat_ax...]
    reduce_scatter x1 -> x0, waiting for transfers between devices: 85 us -> none  [shards(): lax.psum_scatter(terms.astype(jnp.bfloat16), 'ctx', scatter_dimension=1,...]
    all_to_all x1 -> x0, blocking collectives: 62.2 us -> none  [shards(): lax.all_to_all(send_buffer, 'exp', split_axis=0, concat_axis=0, tiled=True)]
    all_to_all x1 -> x0, waiting for transfers between devices: 56.8 us -> none  [shards(): lax.all_to_all(summed, 'exp', split_axis=0, concat_axis=0, tiled=True)]
    dot_general x4 -> x0, matrix products: 35.3 us -> none  [the longest x1 11.6 us: shards(): jnp.einsum('cqhd,ckhd->cqhk', query_heads, key_heads, preferred_element_t...]
    reduce_sum x4 -> x0, other arithmetic: 19.8 us -> none  [the longest x1 8.89 us: shards(): jnp.sum(gate_weights.reshape(token_count, top_count, 1) * expert_out, axi...]
    gather x1 -> x0, local copies, waits for them, and re-layouts: 7.35 us -> none  [shards(): expert_out = returned.reshape(-1, feature_count)[destination]]
  transfers between devices with their start and end apart: 5 -> 0, of which waited for: 5 -> 0; matrix products, arithmetic and copies ran while one was open for 6% -> 0% of each run, Pallas kernels for 0% -> 0%
where the time goes in v1:
time: 203 us; the launch traced here: 202 us
  Pallas kernels  194 us (96%)
  local copies, waits for them, and re-layouts  8.63 us (4%)
    pallas_call x1, Pallas kernels, shards(): pl.pallas_call(functools.partial(layer_kernel, n_exp, cap, chunk, (featur...  194 us
    unnamed x3, local copies, waits for them, and re-layouts  7.16 us

profile of v1, /device:TPU:13, one launch (start us, length us, event | category | flops | bytes accessed | tf_op | source)
XLA Modules:
  0.0 202.3 jit_solution(135293506210601371)
XLA Ops:
  0.0 1.5 copy.10
  1.5 1.5 copy.11.routes_ref
  2.9 3.4 %copy.12 = bf16[256,8,2,256]{3,1,2,0:T(8,128)(2,1)} copy(bf16[256,8,2,256]{3,2,1,0:T(2,128)(2,1)} %bitcast.14) | data formatting | bytes 4194304
  6.3 193.7 %shard_map.91 = bf16[256,2048]{1,0:T(8,128)(2,1)} custom-call(bf16[256,2048]{1,0:T(8,128)(2,1)} %bitcast.20, bf16[256,2048]{1,0:T(8,128)(2,1)} %bitcast.21, bf16[256,2048]{1,0:T(8,128)(2,1)} %bitcast.22, bf16[256,2048]{1,0:T(8,128)(2,1)} %bitcast.23, f32[1,2048]{1,0:T(1,128)} %bitcast.25, s32[256,2]{1,0:T(8,128)} %copy.11.routes_ref, s32[2,256]{1,0:T(2,128)} %bitcast.19, ...), custom_call_target="tpu_custom_call" | custom-call | flops 10000000000 | bytes 20000000 | tf_op jit(solution)/shard_map/pallas_call | solution.py:329
  200.0 2.3 %copy.14 = bf16[1,256,2048]{2,1,0:T(8,128)(2,1)} copy(bf16[1,256,2048]{2,1,0:T(8,128)(2,1)} %bitcast.16) | data formatting | bytes 2097152

commit v2 on v1

--- a/solution.py
+++ b/solution.py
@@ -35,14 +35,14 @@
 
 def layer_kernel(
     n_exp, cap, chunk, scale,
-    q_ref, k_ref, v_ref, residual_ref, gain_ref, routes_ref, routes_t_ref, gates_ref, gu_ref, dn_ref,
+    q_ref, k_ref, v_ref, residual_ref, gain_ref, routes_ref, gates_ref, gu_ref, dn_ref,
     out_ref,
-    q_buf, k_buf, v_buf, residual_buf, mixed, normed, gu_buf, dn_buf,
-    pick, place, send_buf, recv_buf, hidden, result_buf, back_buf,
+    q_buf, k_buf, v_buf, residual_buf, mixed, gu_buf, dn_buf,
+    pick, place, gate_column, send_buf, recv_buf, hidden, result_buf, back_buf,
     local_sem, kv_send, kv_recv, w_send, w_recv, out_send, out_recv, back_send, back_recv,
 ):
     tokens, features = q_ref.shape
-    top = gates_ref.shape[1]
+    top = gates_ref.shape[0]
     units = dn_ref.shape[0]
     slots = send_buf.shape[0]
     chunks = features // chunk
@@ -98,7 +98,7 @@
             device_id_type=MESH,
         )
 
-    gu_pieces, dn_pieces = 4, 2
+    gu_pieces, dn_pieces = 4, features // TILE
     pieces = gu_pieces + dn_pieces
 
     def weight_copy(route, i):
@@ -108,11 +108,10 @@
             src, dst = gu_ref.at[part], gu_buf.at[route, part]
             held = gu_buf.at[CHIP, part]
         else:
-            size = units // dn_pieces
-            start = (i - gu_pieces) * size
-            src = dn_ref.at[pl.ds(start, size)]
-            dst = dn_buf.at[pl.ds(route * units + start, size)]
-            held = dn_buf.at[pl.ds(CHIP * units + start, size)]
+            cols = pl.ds((i - gu_pieces) * TILE, TILE)
+            src = dn_ref.at[:, cols]
+            dst = dn_buf.at[pl.ds(route * units, units), cols]
+            held = dn_buf.at[pl.ds(CHIP * units, units), cols]
         return pltpu.make_async_remote_copy(
             src_ref=held if route == FAR else src,
             dst_ref=dst,
@@ -131,32 +130,48 @@
     for i in range(pieces):
         weight_copy(CORE, i).start()
 
-    expert_lane = lax.broadcasted_iota(jnp.int32, (tokens, 128), 1)
-    named = [routes_ref[:, j : j + 1] == expert_lane for j in range(top)]
+    expert_row = lax.broadcasted_iota(jnp.int32, (128, tokens), 0)
+    named = [routes_ref[j : j + 1, :] == expert_row for j in range(top)]
     counted = sum(jnp.where(hit, 1.0, 0.0) for hit in named).astype(BF16)
     row = lax.broadcasted_iota(jnp.int32, (tokens, tokens), 0)
     col = lax.broadcasted_iota(jnp.int32, (tokens, tokens), 1)
-    earlier = jnp.where(row > col, 1.0, 0.0).astype(BF16)
-    slot = jnp.dot(earlier, counted, preferred_element_type=F32) + (expert_lane * cap).astype(F32)
+    earlier = jnp.where(row < col, 1.0, 0.0).astype(BF16)
+    slot = jnp.dot(counted, earlier, preferred_element_type=F32) + (expert_row * cap).astype(F32)
+    slot_row = lax.broadcasted_iota(jnp.int32, (slots, tokens), 0).astype(F32)
     slot_lane = lax.broadcasted_iota(jnp.int32, (tokens, slots), 1).astype(F32)
-    for j in range(top):
-        target = jnp.sum(jnp.where(named[j], slot, 0.0), axis=1, keepdims=True)
-        pick[j] = jnp.where(target == slot_lane, 1.0, 0.0).astype(BF16)
-
-    expert_row = lax.broadcasted_iota(jnp.int32, (128, tokens), 0)
-    named_t = [routes_t_ref[j : j + 1, :] == expert_row for j in range(top)]
-    counted_t = sum(jnp.where(hit, 1.0, 0.0) for hit in named_t).astype(BF16)
-    earlier_t = jnp.where(row < col, 1.0, 0.0).astype(BF16)
-    slot_t = jnp.dot(counted_t, earlier_t, preferred_element_type=F32) + (expert_row * cap).astype(F32)
-    slot_row = lax.broadcasted_iota(jnp.int32, (slots, tokens), 0).astype(F32)
     placed = jnp.zeros((slots, tokens), F32)
     for j in range(top):
-        target = jnp.sum(jnp.where(named_t[j], slot_t, 0.0), axis=0, keepdims=True)
+        target = jnp.sum(jnp.where(named[j], slot, 0.0), axis=0, keepdims=True)
         placed = placed + jnp.where(target == slot_row, 1.0, 0.0)
+        target = jnp.sum(jnp.where(row == col, target, 0.0), axis=1, keepdims=True)
+        pick[j] = jnp.where(target == slot_lane, 1.0, 0.0).astype(BF16)
+        gate = jnp.sum(jnp.where(row == col, gates_ref[j : j + 1, :], 0.0), axis=1, keepdims=True)
+        gate_column[j] = jnp.broadcast_to(gate, (tokens, 128))
     place[...] = placed.astype(BF16)
 
     for copy in local:
         copy.wait()
+
+    def out_copy(d, cols=slice(None)):
+        return pltpu.make_async_remote_copy(
+            src_ref=send_buf.at[rows_at(flipped(me, d, n_exp) * cap, cap), cols],
+            dst_ref=recv_buf.at[rows_at(d * cap, cap), cols],
+            send_sem=out_send.at[d],
+            recv_sem=out_recv.at[d],
+            device_id={"exp": flipped(me, d, n_exp)},
+            device_id_type=MESH,
+        )
+
+    def back_copy(d, t):
+        cols = columns_at(t, TILE)
+        return pltpu.make_async_remote_copy(
+            src_ref=result_buf.at[rows_at(d * cap, cap), cols],
+            dst_ref=back_buf.at[rows_at(me * cap, cap), cols],
+            send_sem=back_send.at[d, t],
+            recv_sem=back_recv.at[d, t],
+            device_id={"exp": flipped(me, d, n_exp)},
+            device_id_type=MESH,
+        )
 
     @pl.loop(0, chunks + 1)
     def _(g):
@@ -191,100 +206,80 @@
                 weighted = jnp.dot(expo.astype(BF16), v_buf[:, cols], preferred_element_type=F32)
                 mixed[:, cols] = (residual_buf[:, cols].astype(F32) + weighted / total).astype(BF16)
 
-    @pl.loop(0, tokens // 32)
+            cols = columns_at(done, chunk)
+            send_buf[:, cols] = jnp.dot(
+                place[...], mixed[:, cols], preferred_element_type=F32
+            ).astype(BF16)
+
+            @pl.loop(1, n_exp)
+            def _(d):
+                out_copy(n_exp - d, cols).start()
+
+    recv_buf[pl.ds(0, cap), :] = send_buf[rows_at(me * cap, cap), :]
+
+    @pl.loop(1, n_exp)
+    def _(d):
+        out_copy(d).wait_recv()
+
+    @pl.loop(0, slots // 16)
     def _(i):
-        part = rows_at(i * 32, 32)
-        value = mixed[part, :].astype(F32)
+        part = rows_at(i * 16, 16)
+        value = recv_buf[part, :].astype(F32)
         mean_square = jnp.mean(value * value, axis=1, keepdims=True)
-        normed[part, :] = (value * lax.rsqrt(mean_square + 1e-05) * gain_ref[...]).astype(BF16)
-
-    def out_copy(d):
-        return pltpu.make_async_remote_copy(
-            src_ref=send_buf.at[rows_at(flipped(me, d, n_exp) * cap, cap)],
-            dst_ref=recv_buf.at[rows_at(d * cap, cap)],
-            send_sem=out_send.at[d],
-            recv_sem=out_recv.at[d],
-            device_id={"exp": flipped(me, d, n_exp)},
-            device_id_type=MESH,
-        )
-
-    def back_copy(d):
-        return pltpu.make_async_remote_copy(
-            src_ref=result_buf.at[rows_at(d * cap, cap)],
-            dst_ref=back_buf.at[rows_at(me * cap, cap)],
-            send_sem=back_send.at[d],
-            recv_sem=back_recv.at[d],
-            device_id={"exp": flipped(me, d, n_exp)},
-            device_id_type=MESH,
-        )
-
-    my_half = lax.div(me, jnp.int32(half))
-    for which in (1, 0):
-        part = rows_at(lax.rem(my_half + which, jnp.int32(2)) * half_rows, half_rows)
-
-        @pl.loop(0, features // TILE)
-        def _(t):
-            cols = columns_at(t, TILE)
-            send_buf[part, cols] = jnp.dot(
-                place[part, :], normed[:, cols], preferred_element_type=F32
-            ).astype(BF16)
-
-        @pl.loop(max(1, which * half), which * half + half)
-        def _(d):
-            out_copy(d).start()
-
-    recv_buf[pl.ds(0, cap), :] = send_buf[rows_at(me * cap, cap), :]
-
-    for i in range(pieces):
+        recv_buf[part, :] = (value * lax.rsqrt(mean_square + 1e-05) * gain_ref[...]).astype(BF16)
+
+    def expert_hidden(r):
+        both = jnp.dot(recv_buf[...], gu_buf[r], preferred_element_type=F32)
+        gate, up = both[:, :units], both[:, units:]
+        hidden[:, columns_at(r, units)] = (gate / (1.0 + jnp.exp(-gate)) * up).astype(BF16)
+
+    for i in range(gu_pieces):
+        weight_copy(CORE, i).wait_recv()
+    pl.loop(OWN, CHIP)(expert_hidden)
+    for i in range(gu_pieces):
         weight_copy(CHIP, i).wait_recv()
         weight_copy(FAR, i).start()
-    for i in range(pieces):
-        weight_copy(CORE, i).wait_recv()
+    pl.loop(CHIP, CHIP + 1)(expert_hidden)
+    for i in range(gu_pieces):
         weight_copy(FAR, i).wait_recv()
-
-    for which in (0, 1):
-        part = pl.ds(which * half_rows, half_rows)
-
-        @pl.loop(max(1, which * half), which * half + half)
+    pl.loop(FAR, FAR + 1)(expert_hidden)
+
+    for t in range(dn_pieces):
+        weight_copy(CHIP, gu_pieces + t).wait_recv()
+        weight_copy(FAR, gu_pieces + t).start()
+        weight_copy(CORE, gu_pieces + t).wait_recv()
+        weight_copy(FAR, gu_pieces + t).wait_recv()
+        cols = pl.ds(t * TILE, TILE)
+        for which in (1, 0):
+            part = pl.ds(which * half_rows, half_rows)
+            result_buf[part, cols] = jnp.dot(
+                hidden[part, :], dn_buf[:, cols], preferred_element_type=F32
+            ).astype(BF16)
+
+            @pl.loop(max(1, which * half), which * half + half)
+            def _(d):
+                back_copy(d, t).start()
+
+    back_buf[rows_at(me * cap, cap), :] = result_buf[pl.ds(0, cap), :]
+
+    @pl.loop(0, dn_pieces)
+    def _(t):
+        @pl.loop(1, n_exp)
         def _(d):
-            out_copy(d).wait_recv()
-
-        @pl.loop(0, 4)
-        def _(r):
-            both = jnp.dot(recv_buf[part, :], gu_buf[r], preferred_element_type=F32)
-            gate, up = both[:, :units], both[:, units:]
-            hidden[:, columns_at(r, units)] = (gate / (1.0 + jnp.exp(-gate)) * up).astype(BF16)
-
-        @pl.loop(0, features // TILE)
-        def _(t):
-            cols = columns_at(t, TILE)
-            result_buf[part, cols] = jnp.dot(
-                hidden[...], dn_buf[:, cols], preferred_element_type=F32
-            ).astype(BF16)
-
-        @pl.loop(max(1, which * half), which * half + half)
-        def _(d):
-            back_copy(d).start()
-
-    back_buf[rows_at(me * cap, cap), :] = result_buf[pl.ds(0, cap), :]
-
-    @pl.loop(1, n_exp)
-    def _(d):
-        back_copy(d).wait_recv()
-
-    @pl.loop(0, features // TILE)
-    def _(t):
+            back_copy(d, t).wait_recv()
+
         cols = columns_at(t, TILE)
         total = mixed[:, cols].astype(F32)
         for j in range(top):
             routed = jnp.dot(pick[j], back_buf[:, cols], preferred_element_type=F32)
-            total = total + gates_ref[:, j : j + 1] * routed
+            total = total + gate_column[j, :, 0:1] * routed
         out_ref[:, cols] = total.astype(BF16)
 
     @pl.loop(1, n_exp)
     def _(d):
         out_copy(d).wait_send()
-        back_copy(d).wait_send()
+        for t in range(dn_pieces):
+            back_copy(d, t).wait_send()
 
     @pl.loop(0, chunks)
     def _(g):
@@ -321,15 +316,15 @@
     slots = n_exp * cap
     chunk = 256
     chunks = feature_count // chunk
+    tiles = feature_count // TILE
     flat = (tokens, feature_count)
-    flat_routes = routes.reshape(tokens, top)
     anywhere = pl.BlockSpec(memory_space=pl.ANY)
     vmem = pl.BlockSpec(memory_space=pltpu.VMEM)
     dma = pltpu.SemaphoreType.DMA
     out = pl.pallas_call(
         functools.partial(layer_kernel, n_exp, cap, chunk, (feature_count // HEADS) ** (-0.5)),
         out_shape=jax.ShapeDtypeStruct(flat, BF16),
-        in_specs=[anywhere] * 4 + [vmem] * 4 + [anywhere] * 2,
+        in_specs=[anywhere] * 4 + [vmem] * 3 + [anywhere] * 2,
         out_specs=vmem,
         scratch_shapes=[
             pltpu.VMEM(flat, BF16),
@@ -337,25 +332,25 @@
             pltpu.VMEM((n_ctx * tokens, feature_count), BF16),
             pltpu.VMEM(flat, BF16),
             pltpu.VMEM(flat, BF16),
-            pltpu.VMEM(flat, BF16),
             pltpu.VMEM((n_ctx, feature_count, 2 * units), BF16),
             pltpu.VMEM((n_ctx * units, feature_count), BF16),
             pltpu.VMEM((top, tokens, slots), BF16),
             pltpu.VMEM((slots, tokens), BF16),
+            pltpu.VMEM((top, tokens, 128), F32),
             pltpu.VMEM((slots, feature_count), BF16),
             pltpu.VMEM((slots, feature_count), BF16),
-            pltpu.VMEM((slots // 2, n_ctx * units), BF16),
+            pltpu.VMEM((slots, n_ctx * units), BF16),
             pltpu.VMEM((slots, feature_count), BF16),
             pltpu.VMEM((slots, feature_count), BF16),
             dma((6,)),
             dma((2, 3, chunks)),
             dma((2, 3, chunks)),
-            dma((3, 6)),
-            dma((3, 6)),
+            dma((3, 4 + tiles)),
+            dma((3, 4 + tiles)),
             dma((n_exp,)),
             dma((n_exp,)),
-            dma((n_exp,)),
-            dma((n_exp,)),
+            dma((n_exp, tiles)),
+            dma((n_exp, tiles)),
         ],
         compiler_params=pltpu.CompilerParams(
             collective_id=0, has_side_effects=True, vmem_limit_bytes=60 * 1024 * 1024
@@ -369,9 +364,8 @@
         value_rows.reshape(flat),
         residual_in.reshape(flat),
         norm_gain.reshape(1, feature_count),
-        flat_routes,
-        flat_routes.T,
-        gate_weights.reshape(tokens, top),
+        routes.reshape(tokens, top).T,
+        gate_weights.reshape(tokens, top).T,
         gate_up_weight.reshape(feature_count, 2 * units),
         down_weight.reshape(units, feature_count),
     )

time: 203 us -> 172 us (0.85)
  Pallas kernels: 194 us -> 166 us
  local copies, waits for them, and re-layouts: 8.63 us -> 5.69 us
    pallas_call x1, Pallas kernels: 194 us -> 166 us  [shards(): pl.pallas_call(functools.partial(layer_kernel, n_exp, cap, chunk, (featur...]
    unnamed x3 -> x2, local copies, waits for them, and re-layouts: 7.16 us -> 5.69 us
where the time goes in v2:
time: 172 us
  Pallas kernels  166 us (97%)
  local copies, waits for them, and re-layouts  5.69 us (3%)
    pallas_call x1, Pallas kernels, shards(): pl.pallas_call(functools.partial(layer_kernel, n_exp, cap, chunk, (featur...  166 us
    unnamed x2, local copies, waits for them, and re-layouts  5.69 us

profile of v2, /device:TPU:13, one launch (start us, length us, event | category | flops | bytes accessed | tf_op | source)
XLA Modules:
  0.0 171.8 jit_solution(1463128567826846174)
XLA Ops:
  0.0 3.4 %copy.10 = bf16[256,8,2,256]{3,1,2,0:T(8,128)(2,1)} copy(bf16[256,8,2,256]{3,2,1,0:T(2,128)(2,1)} %bitcast.16) | data formatting | bytes 4194304
  3.4 166.1 %shard_map.91 = bf16[256,2048]{1,0:T(8,128)(2,1)} custom-call(bf16[256,2048]{1,0:T(8,128)(2,1)} %bitcast.19, bf16[256,2048]{1,0:T(8,128)(2,1)} %bitcast.20, bf16[256,2048]{1,0:T(8,128)(2,1)} %bitcast.21, bf16[256,2048]{1,0:T(8,128)(2,1)} %bitcast.22, f32[1,2048]{1,0:T(1,128)} %bitcast.24, s32[2,256]{1,0:T(2,128)} %bitcast.25, f32[2,256]{1,0:T(2,128)} %bitcast.26, ...), custom_call_target="tpu_custom_call" | custom-call | flops 10000000000 | bytes 20000000 | tf_op jit(solution)/shard_map/pallas_call | solution.py:324
  169.5 2.3 %copy.12 = bf16[1,256,2048]{2,1,0:T(8,128)(2,1)} copy(bf16[1,256,2048]{2,1,0:T(8,128)(2,1)} %bitcast.18) | data formatting | bytes 2097152

commit v3 on v2

--- a/solution.py
+++ b/solution.py
@@ -37,13 +37,14 @@
     n_exp, cap, chunk, scale,
     q_ref, k_ref, v_ref, residual_ref, gain_ref, routes_ref, gates_ref, gu_ref, dn_ref,
     out_ref,
-    q_buf, k_buf, v_buf, residual_buf, mixed, gu_buf, dn_buf,
+    q_buf, k_buf, v_buf, residual_buf, mixed, raw_buf, gu_buf, dn_buf,
     pick, place, gate_column, send_buf, recv_buf, hidden, result_buf, back_buf,
     local_sem, kv_send, kv_recv, w_send, w_recv, out_send, out_recv, back_send, back_recv,
 ):
     tokens, features = q_ref.shape
     top = gates_ref.shape[0]
     units = dn_ref.shape[0]
+    half_units = units // 2
     slots = send_buf.shape[0]
     chunks = features // chunk
     half = n_exp // 2
@@ -62,7 +63,7 @@
                 (k_ref, k_buf.at[pl.ds(0, tokens)]),
                 (v_ref, v_buf.at[pl.ds(0, tokens)]),
                 (residual_ref, residual_buf),
-                (gu_ref, gu_buf.at[OWN]),
+                (gu_ref, raw_buf),
                 (dn_ref, dn_buf.at[pl.ds(0, units)]),
             ]
         )
@@ -103,10 +104,10 @@
 
     def weight_copy(route, i):
         if i < gu_pieces:
-            size = features // gu_pieces
-            part = pl.ds(i * size, size)
-            src, dst = gu_ref.at[part], gu_buf.at[route, part]
-            held = gu_buf.at[CHIP, part]
+            part = pl.ds(i % 2 * (features // 2), features // 2)
+            cols = pl.ds(i // 2 * units, units)
+            src, dst = gu_buf.at[OWN, part, cols], gu_buf.at[route, part, cols]
+            held = gu_buf.at[CHIP, part, cols]
         else:
             cols = pl.ds((i - gu_pieces) * TILE, TILE)
             src = dn_ref.at[:, cols]
@@ -126,6 +127,18 @@
         for kind in range(2):
             kv_copy(kind, CHIP, g).start()
             kv_copy(kind, CORE, g).start()
+
+    local[4].wait()
+
+    @pl.loop(0, features // 128)
+    def _(i):
+        part = rows_at(i * 128, 128)
+        for j in range(2):
+            value = raw_buf[part, j, :]
+            for h in range(2):
+                gu_buf[OWN, part, h * units + j * half_units : h * units + (j + 1) * half_units] = (
+                    value[:, h * half_units : (h + 1) * half_units]
+                )
 
     for i in range(pieces):
         weight_copy(CORE, i).start()
@@ -149,8 +162,8 @@
         gate_column[j] = jnp.broadcast_to(gate, (tokens, 128))
     place[...] = placed.astype(BF16)
 
-    for copy in local:
-        copy.wait()
+    for i in (0, 1, 2, 3, 5):
+        local[i].wait()
 
     def out_copy(d, cols=slice(None)):
         return pltpu.make_async_remote_copy(
@@ -181,9 +194,10 @@
                 kv_copy(kind, CHIP, g).wait_recv()
                 kv_copy(kind, FAR, g).start()
 
-        @pl.when(g == chunks - 2)
-        def _():
-            for i in range(pieces):
+        for i in range(pieces):
+
+            @pl.when(g == min(2 + i, chunks - 2))
+            def _():
                 weight_copy(CHIP, i).start()
 
         @pl.when(g > 0)
@@ -228,21 +242,30 @@
         mean_square = jnp.mean(value * value, axis=1, keepdims=True)
         recv_buf[part, :] = (value * lax.rsqrt(mean_square + 1e-05) * gain_ref[...]).astype(BF16)
 
-    def expert_hidden(r):
-        both = jnp.dot(recv_buf[...], gu_buf[r], preferred_element_type=F32)
-        gate, up = both[:, :units], both[:, units:]
-        hidden[:, columns_at(r, units)] = (gate / (1.0 + jnp.exp(-gate)) * up).astype(BF16)
+    def expert_hidden(r, h):
+        both = jnp.dot(
+            recv_buf[...], gu_buf[r, :, h * units : (h + 1) * units], preferred_element_type=F32
+        )
+        gate, up = both[:, :half_units], both[:, half_units:]
+        cols = columns_at(2 * r + h, half_units)
+        hidden[:, cols] = (gate / (1.0 + jnp.exp(-gate)) * up).astype(BF16)
 
     for i in range(gu_pieces):
         weight_copy(CORE, i).wait_recv()
-    pl.loop(OWN, CHIP)(expert_hidden)
-    for i in range(gu_pieces):
-        weight_copy(CHIP, i).wait_recv()
-        weight_copy(FAR, i).start()
-    pl.loop(CHIP, CHIP + 1)(expert_hidden)
-    for i in range(gu_pieces):
-        weight_copy(FAR, i).wait_recv()
-    pl.loop(FAR, FAR + 1)(expert_hidden)
+
+    @pl.loop(OWN, CHIP)
+    def _(r):
+        expert_hidden(r, 0)
+        expert_hidden(r, 1)
+
+    for h in range(2):
+        for i in (2 * h, 2 * h + 1):
+            weight_copy(CHIP, i).wait_recv()
+            weight_copy(FAR, i).start()
+        pl.loop(CHIP, CHIP + 1)(functools.partial(expert_hidden, h=h))
+        for i in (2 * h, 2 * h + 1):
+            weight_copy(FAR, i).wait_recv()
+        pl.loop(FAR, FAR + 1)(functools.partial(expert_hidden, h=h))
 
     for t in range(dn_pieces):
         weight_copy(CHIP, gu_pieces + t).wait_recv()
@@ -332,6 +355,7 @@
             pltpu.VMEM((n_ctx * tokens, feature_count), BF16),
             pltpu.VMEM(flat, BF16),
             pltpu.VMEM(flat, BF16),
+            pltpu.VMEM((feature_count, 2, units), BF16),
             pltpu.VMEM((n_ctx, feature_count, 2 * units), BF16),
             pltpu.VMEM((n_ctx * units, feature_count), BF16),
             pltpu.VMEM((top, tokens, slots), BF16),
@@ -366,7 +390,7 @@
         norm_gain.reshape(1, feature_count),
         routes.reshape(tokens, top).T,
         gate_weights.reshape(tokens, top).T,
-        gate_up_weight.reshape(feature_count, 2 * units),
+        gate_up_weight.reshape(feature_count, 2, units),
         down_weight.reshape(units, feature_count),
     )
     return out.reshape(clip_count, row_count, feature_count)

time: 172 us -> 169 us (0.983)
  local copies, waits for them, and re-layouts: 5.69 us -> 2.3 us
    unnamed x2 -> x1, local copies, waits for them, and re-layouts: 5.69 us -> 2.3 us
where the time goes in v3:
time: 169 us; the launch traced here: 168 us
  Pallas kernels  166 us (98%)
  local copies, waits for them, and re-layouts  2.3 us (1%)
    pallas_call x1, Pallas kernels, shards(): pl.pallas_call(functools.partial(layer_kernel, n_exp, cap, chunk, (featur...  166 us

profile of v3, /device:TPU:13, one launch (start us, length us, event | category | flops | bytes accessed | tf_op | source)
XLA Modules:
  0.0 168.4 jit_solution(13217431077772555697)
XLA Ops:
  0.0 166.1 %shard_map.91 = bf16[256,2048]{1,0:T(8,128)(2,1)} custom-call(bf16[256,2048]{1,0:T(8,128)(2,1)} %bitcast.16, bf16[256,2048]{1,0:T(8,128)(2,1)} %bitcast.17, bf16[256,2048]{1,0:T(8,128)(2,1)} %bitcast.18, bf16[256,2048]{1,0:T(8,128)(2,1)} %bitcast.19, f32[1,2048]{1,0:T(1,128)} %bitcast.21, s32[2,256]{1,0:T(2,128)} %bitcast.22, f32[2,256]{1,0:T(2,128)} %bitcast.23, ...), custom_call_target="tpu_custom_call" | custom-call | flops 10000000000 | bytes 20000000 | tf_op jit(solution)/shard_map/pallas_call | solution.py:347
  166.1 2.3 %copy.11 = bf16[1,256,2048]{2,1,0:T(8,128)(2,1)} copy(bf16[1,256,2048]{2,1,0:T(8,128)(2,1)} %bitcast.14) | data formatting | bytes 2097152

commit v4 on v3

--- a/solution.py
+++ b/solution.py
@@ -13,6 +13,7 @@
 BF16 = jnp.bfloat16
 OWN, CORE, CHIP, FAR = range(4)
 TILE = 512
+AHEAD = 3
 
 
 def flipped(index, offset, extent):
@@ -122,10 +123,14 @@
             device_id_type=MESH,
         )
 
+    @pl.loop(0, AHEAD)
+    def _(g):
+        for kind in range(2):
+            kv_copy(kind, CHIP, g).start()
+
     @pl.loop(0, chunks)
     def _(g):
         for kind in range(2):
-            kv_copy(kind, CHIP, g).start()
             kv_copy(kind, CORE, g).start()
 
     local[4].wait()
@@ -194,9 +199,14 @@
                 kv_copy(kind, CHIP, g).wait_recv()
                 kv_copy(kind, FAR, g).start()
 
-        for i in range(pieces):
-
-            @pl.when(g == min(2 + i, chunks - 2))
+        @pl.when(g + AHEAD < chunks)
+        def _():
+            for kind in range(2):
+                kv_copy(kind, CHIP, g + AHEAD).start()
+
+        for i in range(AHEAD):
+
+            @pl.when(g == chunks - AHEAD + i)
             def _():
                 weight_copy(CHIP, i).start()
 
@@ -229,6 +239,15 @@
             def _(d):
                 out_copy(n_exp - d, cols).start()
 
+    def weight_step(i, following):
+        weight_copy(CHIP, i).wait_recv()
+        weight_copy(FAR, i).start()
+        for n in following:
+            weight_copy(CHIP, n).start()
+
+    weight_step(0, [3])
+    weight_step(1, [])
+
     recv_buf[pl.ds(0, cap), :] = send_buf[rows_at(me * cap, cap), :]
 
     @pl.loop(1, n_exp)
@@ -259,9 +278,9 @@
         expert_hidden(r, 1)
 
     for h in range(2):
-        for i in (2 * h, 2 * h + 1):
-            weight_copy(CHIP, i).wait_recv()
-            weight_copy(FAR, i).start()
+        if h == 1:
+            weight_step(2, [gu_pieces])
+            weight_step(3, range(gu_pieces + 1, pieces))
         pl.loop(CHIP, CHIP + 1)(functools.partial(expert_hidden, h=h))
         for i in (2 * h, 2 * h + 1):
             weight_copy(FAR, i).wait_recv()

time: 169 us -> 169 us (level)
  no operation moved by 1% of the time
where the time goes in v4:
time: 169 us; the launch traced here: 168 us
  Pallas kernels  166 us (98%)
  local copies, waits for them, and re-layouts  2.3 us (1%)
    pallas_call x1, Pallas kernels, shards(): pl.pallas_call(functools.partial(layer_kernel, n_exp, cap, chunk, (featur...  166 us

profile of v4, /device:TPU:13, one launch (start us, length us, event | category | flops | bytes accessed | tf_op | source)
XLA Modules:
  0.0 168.4 jit_solution(5579105969683071388)
XLA Ops:
  0.0 166.1 %shard_map.91 = bf16[256,2048]{1,0:T(8,128)(2,1)} custom-call(bf16[256,2048]{1,0:T(8,128)(2,1)} %bitcast.16, bf16[256,2048]{1,0:T(8,128)(2,1)} %bitcast.17, bf16[256,2048]{1,0:T(8,128)(2,1)} %bitcast.18, bf16[256,2048]{1,0:T(8,128)(2,1)} %bitcast.19, f32[1,2048]{1,0:T(1,128)} %bitcast.21, s32[2,256]{1,0:T(2,128)} %bitcast.22, f32[2,256]{1,0:T(2,128)} %bitcast.23, ...), custom_call_target="tpu_custom_call" | custom-call | flops 10000000000 | bytes 20000000 | tf_op jit(solution)/shard_map/pallas_call | solution.py:366
  166.1 2.3 %copy.11 = bf16[1,256,2048]{2,1,0:T(8,128)(2,1)} copy(bf16[1,256,2048]{2,1,0:T(8,128)(2,1)} %bitcast.14) | data formatting | bytes 2097152

commit v5 on v4

--- a/solution.py
+++ b/solution.py
@@ -254,9 +254,9 @@
     def _(d):
         out_copy(d).wait_recv()
 
-    @pl.loop(0, slots // 16)
+    @pl.loop(0, slots // 32)
     def _(i):
-        part = rows_at(i * 16, 16)
+        part = rows_at(i * 32, 32)
         value = recv_buf[part, :].astype(F32)
         mean_square = jnp.mean(value * value, axis=1, keepdims=True)
         recv_buf[part, :] = (value * lax.rsqrt(mean_square + 1e-05) * gain_ref[...]).astype(BF16)
@@ -286,21 +286,27 @@
             weight_copy(FAR, i).wait_recv()
         pl.loop(FAR, FAR + 1)(functools.partial(expert_hidden, h=h))
 
+    def send_results(which, t):
+        part = pl.ds(which * half_rows, half_rows)
+        cols = columns_at(t, TILE)
+        result_buf[part, cols] = jnp.dot(
+            hidden[part, :], dn_buf[:, cols], preferred_element_type=F32
+        ).astype(BF16)
+
+        @pl.loop(max(1, which * half), which * half + half)
+        def _(d):
+            back_copy(d, t).start()
+
     for t in range(dn_pieces):
         weight_copy(CHIP, gu_pieces + t).wait_recv()
         weight_copy(FAR, gu_pieces + t).start()
         weight_copy(CORE, gu_pieces + t).wait_recv()
         weight_copy(FAR, gu_pieces + t).wait_recv()
-        cols = pl.ds(t * TILE, TILE)
-        for which in (1, 0):
-            part = pl.ds(which * half_rows, half_rows)
-            result_buf[part, cols] = jnp.dot(
-                hidden[part, :], dn_buf[:, cols], preferred_element_type=F32
-            ).astype(BF16)
-
-            @pl.loop(max(1, which * half), which * half + half)
-            def _(d):
-                back_copy(d, t).start()
+        send_results(1, t)
+
+    @pl.loop(0, dn_pieces)
+    def _(t):
+        send_results(0, t)
 
     back_buf[rows_at(me * cap, cap), :] = result_buf[pl.ds(0, cap), :]
 

time: 169 us -> 169 us (level)
  no operation moved by 1% of the time
where the time goes in v5:
time: 169 us
  Pallas kernels  167 us (99%)
  local copies, waits for them, and re-layouts  2.3 us (1%)
    pallas_call x1, Pallas kernels, shards(): pl.pallas_call(functools.partial(layer_kernel, n_exp, cap, chunk, (featur...  167 us

profile of v5, /device:TPU:13, one launch (start us, length us, event | category | flops | bytes accessed | tf_op | source)
XLA Modules:
  0.0 168.8 jit_solution(12388893175256776538)
XLA Ops:
  0.0 166.5 %shard_map.91 = bf16[256,2048]{1,0:T(8,128)(2,1)} custom-call(bf16[256,2048]{1,0:T(8,128)(2,1)} %bitcast.16, bf16[256,2048]{1,0:T(8,128)(2,1)} %bitcast.17, bf16[256,2048]{1,0:T(8,128)(2,1)} %bitcast.18, bf16[256,2048]{1,0:T(8,128)(2,1)} %bitcast.19, f32[1,2048]{1,0:T(1,128)} %bitcast.21, s32[2,256]{1,0:T(2,128)} %bitcast.22, f32[2,256]{1,0:T(2,128)} %bitcast.23, ...), custom_call_target="tpu_custom_call" | custom-call | flops 10000000000 | bytes 20000000 | tf_op jit(solution)/shard_map/pallas_call | solution.py:372
  166.5 2.3 %copy.11 = bf16[1,256,2048]{2,1,0:T(8,128)(2,1)} copy(bf16[1,256,2048]{2,1,0:T(8,128)(2,1)} %bitcast.14) | data formatting | bytes 2097152
